TPU v7x, 32 devices: a whole 2x2x4 slice. The times are simulated.
32 devices in a mesh: patch: 8 (over y, x, core), slab: 4 (over z).
Axes of the slice: x: 2, y: 2, z: 4, core: 2. Of those that a mesh axis runs over, the one named last changes fastest.
Arguments:
- history: bfloat16 [128, 256, 128], P('patch', 'slab'), may hold values from -6 to 6
- interp_weights: bfloat16 [128, 32, 4], P('patch'), may hold values from -3 to 3
- pair_table: int32 [128, 32, 3], P('patch'), may hold values from 0 to 252, as said below
- coupling: bfloat16 [128, 32, 128, 128], P('patch', 'slab'), may hold values from -0.09375 to 0.09375
- self_inverse: bfloat16 [128, 128, 128], P('patch'), may hold values from -0.5 to 0.5
- incident: float32 [128, 4, 128], P('patch'), may hold values from -6 to 6
Outputs:
- amplitudes: bfloat16 [128, 4, 128], P('patch')
Inputs may be any that keep to these rules, and one draw needn't show every extreme that they name: pair_table[p, k] holds the observer patch (0 to 127), the first delay step (1 to 252) and the band width (1 to 4) of the k-th interaction whose sources are patch p's.
All inputs are finite; a program needn't handle non-finite values.
Results may differ from a plain program's by a relative error of at most 0.008.
Values may be sent and summed in bfloat16 or wider, within the bound.
A program may use at most 64 MiB of HBM per device.

v0:
```python
import jax
import jax.numpy as jnp
from jax import lax
from jax.sharding import PartitionSpec as P

WMAX = 4
STEPS = 4


def on_device(history, interp_weights, pair_table, coupling, self_inverse, incident):
    patch_dev = history.shape[0]
    slab_len = history.shape[1]
    src_count = history.shape[2]
    local_pairs = coupling.shape[1]
    slab_id = lax.axis_index("slab")
    observer = pair_table[:, :, 0]
    first_delay = pair_table[:, :, 1]
    band_width = pair_table[:, :, 2]
    tap_index = jnp.arange(WMAX, dtype=jnp.int32)
    weights = jnp.where(
        tap_index[None, None, :] < band_width[:, :, None],
        interp_weights,
        jnp.zeros_like(interp_weights),
    )
    slab_rows = jnp.arange(slab_len, dtype=jnp.int32)
    pair_start = slab_id * local_pairs
    local_delay = lax.dynamic_slice_in_dim(first_delay, pair_start, local_pairs, 1)
    local_weights = lax.dynamic_slice_in_dim(weights, pair_start, local_pairs, 1)
    local_obs = lax.dynamic_slice_in_dim(observer, pair_start, local_pairs, 1).reshape(-1)
    step_rows = jnp.arange(STEPS, dtype=jnp.int32)
    new_amps = jnp.zeros((patch_dev, STEPS, src_count), jnp.bfloat16)
    for time_step in range(STEPS):
        step_list = jnp.full((1,), time_step, jnp.int32)
        target = first_delay[:, :, None] + tap_index[None, None, :] - 1 - slab_id * slab_len
        rows_hit = target[:, :, None, :] - step_list[None, None, :, None]
        onehot = rows_hit[..., None] == slab_rows
        tables = jnp.sum(
            jnp.where(onehot, weights[:, :, None, :, None], jnp.zeros((), jnp.bfloat16)), axis=3
        )
        stored = lax.psum_scatter(
            jnp.einsum("pcsl,plj->cpsj", tables, history, preferred_element_type=jnp.float32),
            "slab",
            scatter_dimension=0,
            tiled=True,
        )[:, :, 0]
        recent_time = time_step - local_delay[:, :, None] - tap_index[None, None, :]
        recent_hit = recent_time[..., None] == step_rows
        recent_table = jnp.sum(
            jnp.where(recent_hit, local_weights[..., None], jnp.zeros((), jnp.bfloat16)), axis=2
        )
        recent = jnp.einsum(
            "pkm,pmj->kpj", recent_table, new_amps, preferred_element_type=jnp.float32
        )
        driven = (stored + recent).astype(jnp.bfloat16)
        coupled = jnp.einsum("pkij,kpj->pki", coupling, driven, preferred_element_type=jnp.float32)
        contrib = coupled.reshape(-1, src_count)
        targets = jnp.arange(patch_dev * lax.axis_size("patch"), dtype=jnp.int32)
        field_onehot = (targets[:, None] == local_obs[None, :]).astype(jnp.float32)
        field_share = lax.psum_scatter(
            jnp.dot(
                field_onehot,
                contrib,
                precision=lax.Precision.HIGHEST,
                preferred_element_type=jnp.float32,
            ),
            "patch",
            scatter_dimension=0,
            tiled=True,
        )
        scattered = lax.psum(field_share, "slab")
        drive = (incident[:, time_step] - scattered).astype(jnp.bfloat16)
        amplitude = jnp.einsum(
            "pij,pj->pi", self_inverse, drive, preferred_element_type=jnp.float32
        ).astype(jnp.bfloat16)
        new_amps = new_amps.at[:, time_step].set(amplitude)
    return new_amps


def solution(mesh):
    in_specs = (
        P("patch", "slab", None),
        P("patch", None, None),
        P("patch", None, None),
        P("patch", "slab", None, None),
        P("patch", None, None),
        P("patch", None, None),
    )
    out_specs = P("patch", None, None)
    return jax.shard_map(
        on_device, mesh=mesh, in_specs=in_specs, out_specs=out_specs, check_vma=False
    )
```

profile of v0, /device:TPU:0, one launch (start us, length us, event | category | flops | bytes accessed | tf_op | source)
XLA Modules:
  0.0 272.6 jit_solution(6054449320401630764)
XLA Ops:
  6.6 0.8 fusion.62
  7.4 0.7 fusion.44
  8.1 2.1 fusion.16
  10.2 1.8 convolution_bitcast_fusion.3
  12.1 0.0 reduce-scatter.9.cloned.1.call-update
  12.1 0.0 reduce-scatter.11.cloned.1.call-start
  12.1 0.1 constant_dynamic-slice_fusion.1
  12.2 0.1 copy.61
  12.3 0.1 constant_dynamic-slice_fusion
  12.4 0.1 copy.27
  12.5 0.1 copy.28
  12.6 0.1 constant_dynamic-slice_fusion.2
  12.7 0.1 eq.173
  12.8 21.7 %reduce-scatter.9.cloned.1.call-done = f32[8,16,1,128]{3,0,1,2:T(8,128)} async-done(((f32[32,16,1,128]{3,0,1,2:T(8,128)}), f32[8,16,1,128]{3,0,1,2:T(8,128)}) %reduce-scatter.9.cloned.1.call-update) | async-done | bytes 65552 | tf_op jit(solution)/shard_map/reduce_scatter | solution.py:40
  34.5 1.0 fusion.11
  35.6 4.4 %fusion.26 = f32[16,8,1,128]{3,2,1,0:T(1,128)S(1)} fusion(bf16[16,8,128,128]{3,2,1,0:T(8,128)(2,1)} %param.17, bf16[8,16,128,1]{2,0,1,3:T(8,128)(2,1)S(1)} %fusion.11), kind=kOutput, calls=%fused_computation.38 | convolution fusion | flops 4194304 | bytes 4292608 | tf_op jit(solution)/shard_map/pkij,kpj->pki/dot_general | solution.py:55
  40.0 0.8 fusion.31
  40.8 0.0 reduce-scatter.11.cloned.1.call-update
  40.9 0.0 reduce-scatter.13.cloned.1.call-start
  40.9 0.9 convolution_bitcast_fusion.2
  41.8 0.0 reduce-scatter.13.cloned.1.call-update
  41.8 0.0 reduce-scatter.15.cloned.1.call-start
  41.9 0.1 copy.31
  42.0 30.5 %reduce-scatter.11.cloned.1.call-done = f32[16,128]{1,0:T(8,128)} async-done(((f32[128,128]{1,0:T(8,128)}), f32[16,128]{1,0:T(8,128)}) %reduce-scatter.11.cloned.1.call-update) | async-done | bytes 8208 | tf_op jit(solution)/shard_map/reduce_scatter | solution.py:59
  72.5 12.1 %psum.28 = f32[16,128]{1,0:T(8,128)S(1)} all-reduce(f32[16,128]{1,0:T(8,128)} %reduce-scatter.11.cloned.1.call-done), channel_id=1, replica_groups=mesh['patch'=8,'slab'=4] {'slab'}, use_global_device_ids=true, to_apply=%region_4.5 | all-reduce | flops 2048 | bytes 16384 | tf_op jit(solution)/shard_map/psum | solution.py:70
  84.6 0.4 fusion.51
  85.0 9.5 %reduce-scatter.13.cloned.1.call-done = f32[8,16,1,128]{3,0,1,2:T(8,128)} async-done(((f32[32,16,1,128]{3,0,1,2:T(8,128)}), f32[8,16,1,128]{3,0,1,2:T(8,128)}) %reduce-scatter.13.cloned.1.call-update) | async-done | bytes 65552 | tf_op jit(solution)/shard_map/reduce_scatter | solution.py:40
  94.5 1.0 fusion.10
  95.5 4.4 %fusion.24 = f32[16,8,1,128]{3,2,1,0:T(1,128)S(1)} fusion(bf16[16,8,128,128]{3,2,1,0:T(8,128)(2,1)} %param.17, bf16[8,16,128,1]{2,0,1,3:T(8,128)(2,1)S(1)} %fusion.10), kind=kOutput, calls=%fused_computation.36 | convolution fusion | flops 4194304 | bytes 4292608 | tf_op jit(solution)/shard_map/pkij,kpj->pki/dot_general | solution.py:55
  99.9 0.8 fusion.30
  100.8 0.0 reduce-scatter.15.cloned.1.call-update
  100.8 0.0 reduce-scatter.17.cloned.1.call-start
  100.9 0.9 convolution_bitcast_fusion.1
  101.7 0.0 reduce-scatter.17.cloned.1.call-update
  101.8 0.0 reduce-scatter.19.cloned.1.call-start
  101.8 0.1 copy.34
  101.9 30.5 %reduce-scatter.15.cloned.1.call-done = f32[16,128]{1,0:T(8,128)} async-done(((f32[128,128]{1,0:T(8,128)}), f32[16,128]{1,0:T(8,128)}) %reduce-scatter.15.cloned.1.call-update) | async-done | bytes 8208 | tf_op jit(solution)/shard_map/reduce_scatter | solution.py:59
  132.4 12.0 %psum.29 = f32[16,128]{1,0:T(8,128)S(1)} all-reduce(f32[16,128]{1,0:T(8,128)} %reduce-scatter.15.cloned.1.call-done), channel_id=1, replica_groups=mesh['patch'=8,'slab'=4] {'slab'}, use_global_device_ids=true, to_apply=%region_9.10 | all-reduce | flops 2048 | bytes 16384 | tf_op jit(solution)/shard_map/psum | solution.py:70
  144.4 0.4 fusion.49
  144.8 0.1 scatter.15
  144.8 9.3 %reduce-scatter.17.cloned.1.call-done = f32[8,16,1,128]{3,0,1,2:T(8,128)} async-done(((f32[32,16,1,128]{3,0,1,2:T(8,128)}), f32[8,16,1,128]{3,0,1,2:T(8,128)}) %reduce-scatter.17.cloned.1.call-update) | async-done | bytes 65552 | tf_op jit(solution)/shard_map/reduce_scatter | solution.py:40
  154.1 1.0 fusion.9
  155.2 4.4 %fusion.22 = f32[16,8,1,128]{3,2,1,0:T(1,128)S(1)} fusion(bf16[16,8,128,128]{3,2,1,0:T(8,128)(2,1)} %param.17, bf16[8,16,128,1]{2,0,1,3:T(8,128)(2,1)S(1)} %fusion.9), kind=kOutput, calls=%fused_computation.34 | convolution fusion | flops 4194304 | bytes 4292608 | tf_op jit(solution)/shard_map/pkij,kpj->pki/dot_general | solution.py:55
  159.6 0.8 fusion.29
  160.5 0.0 reduce-scatter.19.cloned.1.call-update
  160.5 0.0 reduce-scatter.21.cloned.1.call-start
  160.5 0.9 convolution_bitcast_fusion
  161.4 0.0 reduce-scatter.21.cloned.1.call-update
  161.4 0.0 reduce-scatter.23.cloned.1.call-start
  161.5 0.1 copy.37
  161.6 30.5 %reduce-scatter.19.cloned.1.call-done = f32[16,128]{1,0:T(8,128)} async-done(((f32[128,128]{1,0:T(8,128)}), f32[16,128]{1,0:T(8,128)}) %reduce-scatter.19.cloned.1.call-update) | async-done | bytes 8208 | tf_op jit(solution)/shard_map/reduce_scatter | solution.py:59
  192.1 12.1 %psum.30 = f32[16,128]{1,0:T(8,128)S(1)} all-reduce(f32[16,128]{1,0:T(8,128)} %reduce-scatter.19.cloned.1.call-done), channel_id=1, replica_groups=mesh['patch'=8,'slab'=4] {'slab'}, use_global_device_ids=true, to_apply=%region_14.15 | all-reduce | flops 2048 | bytes 16384 | tf_op jit(solution)/shard_map/psum | solution.py:70
  204.2 0.4 fusion.47
  204.6 0.1 scatter.16
  204.7 0.0 copy-start.2
  204.7 9.4 %reduce-scatter.21.cloned.1.call-done = f32[8,16,1,128]{3,0,1,2:T(8,128)} async-done(((f32[32,16,1,128]{3,0,1,2:T(8,128)}), f32[8,16,1,128]{3,0,1,2:T(8,128)}) %reduce-scatter.21.cloned.1.call-update) | async-done | bytes 65552 | tf_op jit(solution)/shard_map/reduce_scatter | solution.py:40
  214.1 1.0 fusion.8
  215.1 4.4 %fusion.20 = f32[16,8,1,128]{3,2,1,0:T(1,128)S(1)} fusion(bf16[16,8,128,128]{3,2,1,0:T(8,128)(2,1)} %param.17, bf16[8,16,128,1]{2,0,1,3:T(8,128)(2,1)S(1)} %fusion.8), kind=kOutput, calls=%fused_computation.32 | convolution fusion | flops 4194304 | bytes 4292608 | tf_op jit(solution)/shard_map/pkij,kpj->pki/dot_general | solution.py:55
  219.6 0.8 fusion.28
  220.4 0.0 reduce-scatter.23.cloned.1.call-update
  220.4 31.6 %reduce-scatter.23.cloned.1.call-done = f32[16,128]{1,0:T(8,128)} async-done(((f32[128,128]{1,0:T(8,128)}), f32[16,128]{1,0:T(8,128)}) %reduce-scatter.23.cloned.1.call-update) | async-done | bytes 8208 | tf_op jit(solution)/shard_map/reduce_scatter | solution.py:59
  252.0 12.0 %psum.31 = f32[16,128]{1,0:T(8,128)S(1)} all-reduce(f32[16,128]{1,0:T(8,128)} %reduce-scatter.23.cloned.1.call-done), channel_id=1, replica_groups=mesh['patch'=8,'slab'=4] {'slab'}, use_global_device_ids=true, to_apply=%region_19.20 | all-reduce | flops 2048 | bytes 16384 | tf_op jit(solution)/shard_map/psum | solution.py:70
  264.0 0.4 fusion.45
  264.4 1.4 scatter.19
  (27 shorter events, 0.3 us)
Async XLA Ops:
  6.5 78.0 %copy-start = (bf16[16,128,128]{2,1,0:T(8,128)(2,1)S(1)}, bf16[16,128,128]{2,1,0:T(8,128)(2,1)}, u32[]{:S(2)}) copy-start(bf16[16,128,128]{2,1,0:T(8,128)(2,1)} %param.18) | copy-start | bytes 1572868
  6.5 34.4 %copy-start.1 = (bf16[16,64,128]{2,1,0:T(8,128)(2,1)S(1)}, bf16[16,64,128]{2,1,0:T(8,128)(2,1)}, u32[]{:S(2)}) copy-start(bf16[16,64,128]{2,1,0:T(8,128)(2,1)} %param.14) | copy-start | bytes 786436
  6.5 35.3 %copy-start.3 = (f32[16,4,128]{2,1,0:T(4,128)S(1)}, f32[16,4,128]{2,1,0:T(4,128)}, u32[]{:S(2)}) copy-start(f32[16,4,128]{2,1,0:T(4,128)} %param.19) | copy-start | bytes 98308
  6.5 28.0 %reduce-scatter.9.cloned.1.call-start = ((), (), s32[]{:S(2)}) async-start(), calls=%async_computation.8 | async-start | bytes 327680 | tf_op jit(solution)/shard_map/reduce_scatter | solution.py:40
  12.1 60.4 %reduce-scatter.11.cloned.1.call-start = ((), (), s32[]{:S(2)}) async-start(), calls=%async_computation.9 | async-start | bytes 73728 | tf_op jit(solution)/shard_map/reduce_scatter | solution.py:59
  40.9 53.6 %reduce-scatter.13.cloned.1.call-start = ((), (), s32[]{:S(2)}) async-start(), calls=%async_computation.10 | async-start | bytes 327680 | tf_op jit(solution)/shard_map/reduce_scatter | solution.py:40
  41.8 90.6 %reduce-scatter.15.cloned.1.call-start = ((), (), s32[]{:S(2)}) async-start(), calls=%async_computation.11 | async-start | bytes 73728 | tf_op jit(solution)/shard_map/reduce_scatter | solution.py:59
  100.8 53.3 %reduce-scatter.17.cloned.1.call-start = ((), (), s32[]{:S(2)}) async-start(), calls=%async_computation.12 | async-start | bytes 327680 | tf_op jit(solution)/shard_map/reduce_scatter | solution.py:40
  101.8 90.4 %reduce-scatter.19.cloned.1.call-start = ((), (), s32[]{:S(2)}) async-start(), calls=%async_computation.13 | async-start | bytes 73728 | tf_op jit(solution)/shard_map/reduce_scatter | solution.py:59
  160.5 53.6 %reduce-scatter.21.cloned.1.call-start = ((), (), s32[]{:S(2)}) async-start(), calls=%async_computation.14 | async-start | bytes 327680 | tf_op jit(solution)/shard_map/reduce_scatter | solution.py:40
  161.4 90.6 %reduce-scatter.23.cloned.1.call-start = ((), (), s32[]{:S(2)}) async-start(), calls=%async_computation.15 | async-start | bytes 73728 | tf_op jit(solution)/shard_map/reduce_scatter | solution.py:59
  204.7 59.7 %copy-start.2 = (bf16[16,4,128]{2,1,0:T(4,128)(2,1)}, bf16[16,4,128]{2,1,0:T(4,128)(2,1)S(1)}, u32[]{:S(2)}) copy-start(bf16[16,4,128]{2,1,0:T(4,128)(2,1)S(1)} %scatter.16) | copy-start | bytes 49156
Sparse Core Ops, SparseCore 0:
  12.2 22.2 reduce-scatter.8
  41.0 31.4 reduce-scatter.10
  74.8 19.6 reduce-scatter.12
  100.9 31.4 reduce-scatter.14
  134.5 19.6 reduce-scatter.16
  160.6 31.4 reduce-scatter.18
  194.4 19.6 reduce-scatter.20
  220.5 31.4 reduce-scatter.22
where the time goes:
time: 273 us
  waiting for transfers between devices  173 us (63%)
  blocking collectives  48 us (18%)
  matrix products  31.2 us (11%)
  between operations  13.7 us (5%)
  local copies, waits for them, and re-layouts  3.27 us (1%)
  other arithmetic  2.94 us (1%)
    reduce_scatter x4, waiting for transfers between devices, on_device(): lax.psum_scatter(jnp.dot(field_onehot, contrib, precision=lax.Precision.H...  123 us
    reduce_scatter x4, waiting for transfers between devices, on_device(): lax.psum_scatter(jnp.einsum('pcsl,plj->cpsj', tables, history, preferred_...  50 us
    psum x4, blocking collectives, on_device(): scattered = lax.psum(field_share, 'slab')  48 us
    dot_general x4, matrix products, on_device(): jnp.einsum('pkij,kpj->pki', coupling, driven, preferred_element_type=jnp....  17.7 us
  transfers between devices with their start and end apart: 8, of which 8 were waited for; matrix products, arithmetic and copies ran while one was open for 2% of the time, Pallas kernels for 0%

commit v1 on v0

v1 whole, which is shorter than its diff:
```python
import functools

import jax
import jax.numpy as jnp
from jax import lax
from jax.experimental import pallas as pl
from jax.experimental.pallas import tpu as pltpu
from jax.sharding import PartitionSpec as P

WMAX = 4
STEPS = 4
MESH = pl.DeviceIdType.MESH
F32 = jnp.float32
BF16 = jnp.bfloat16


def nt_dot(x, m):
    return lax.dot_general(x, m, (((1,), (1,)), ((), ())), preferred_element_type=F32)


def own_blocks(x, m):
    rows, src = x.shape
    full = nt_dot(x.astype(BF16), m)
    row = lax.broadcasted_iota(jnp.int32, (rows, src), 0)
    out = full[:, :src]
    for r in range(1, rows):
        out = jnp.where(row == r, full[:, r * src : (r + 1) * src], out)
    return out


def march(
    n_patch,
    n_slab,
    hist_ref,
    w_ref,
    pt_ref,
    coup_hbm,
    inv_hbm,
    inc_ref,
    out_ref,
    coup,
    inv,
    wm,
    recent_w,
    onehot,
    inc,
    amps,
    pre,
    coupled,
    hsend,
    hrecv,
    fsend,
    frecv,
    zbuf,
    local_sem,
    h_send_sem,
    h_recv_sem,
    f_send_sem,
    f_recv_sem,
    z_send_sem,
    z_recv_sem,
):
    patches, slab_len, src = hist_ref.shape
    pairs = pt_ref.shape[1]
    loc = pairs // n_slab
    rows = patches * loc
    total = n_patch * patches
    me = lax.axis_index("patch")
    slab = lax.axis_index("slab")

    def patch_peer(off):
        return lax.rem(me + off, n_patch)

    def slab_peer(off):
        return lax.rem(slab + off, n_slab)

    barrier = pltpu.get_barrier_semaphore()
    for off in range(1, n_patch):
        pl.semaphore_signal(
            barrier, inc=1, device_id={"patch": patch_peer(off), "slab": slab}, device_id_type=MESH
        )
    for off in range(1, n_slab):
        pl.semaphore_signal(
            barrier, inc=1, device_id={"patch": me, "slab": slab_peer(off)}, device_id_type=MESH
        )

    parts = 4
    size = patches // parts
    loads = [
        pltpu.make_async_copy(
            coup_hbm.at[pl.ds(c * size, size)], coup.at[pl.ds(c * size, size)], local_sem.at[c]
        )
        for c in range(parts)
    ]
    loads.append(pltpu.make_async_copy(inv_hbm, inv, local_sem.at[parts]))
    for load in loads:
        load.start()

    lane = lax.broadcasted_iota(jnp.int32, (pairs, slab_len), 1) + (slab * slab_len + 1)
    tap = lax.broadcasted_iota(jnp.int32, (pairs, WMAX), 1)

    def stored_share(p, steps):
        table = pt_ref[p]
        weights = wm[p]
        shift = lane - table[:, 1:2]
        hits = []
        for step in steps:
            hit = jnp.zeros((pairs, slab_len), F32)
            for j in range(WMAX):
                hit = jnp.where(shift == j - step, weights[:, j : j + 1], hit)
            hits.append(hit)
        hit = hits[0] if len(hits) == 1 else jnp.concatenate(hits, axis=0)
        return jnp.dot(hit.astype(BF16), hist_ref[p], preferred_element_type=F32)

    def share_of_steps(steps):
        def two(i, carry):
            a = stored_share(2 * i, steps)
            b = stored_share(2 * i + 1, steps)
            at = pl.ds(pl.multiple_of(i * 2 * loc, 2 * loc), 2 * loc)
            for k, step in enumerate(steps):
                for d in range(n_slab):
                    r = k * pairs + d * loc
                    both = jnp.concatenate([a[r : r + loc], b[r : r + loc]], axis=0)
                    hsend[step, d, at, :] = both.astype(BF16)
            return carry

        lax.fori_loop(0, patches // 2, two, 0, unroll=True)

    def hist_copy(step, off):
        dest = slab_peer(off)
        return pltpu.make_async_remote_copy(
            src_ref=hsend.at[step, dest],
            dst_ref=hrecv.at[step, off],
            send_sem=h_send_sem.at[step, off],
            recv_sem=h_recv_sem.at[step, off],
            device_id={"patch": me, "slab": dest},
            device_id_type=MESH,
        )

    def field_copy(step, off):
        dest = patch_peer(off)
        return pltpu.make_async_remote_copy(
            src_ref=fsend.at[step, dest],
            dst_ref=frecv.at[step, off],
            send_sem=f_send_sem.at[step, off],
            recv_sem=f_recv_sem.at[step, off],
            device_id={"patch": dest, "slab": slab},
            device_id_type=MESH,
        )

    def slab_copy(step, off):
        return pltpu.make_async_remote_copy(
            src_ref=zbuf.at[step, 0],
            dst_ref=zbuf.at[step, off],
            send_sem=z_send_sem.at[step, off],
            recv_sem=z_recv_sem.at[step, off],
            device_id={"patch": me, "slab": slab_peer(off)},
            device_id_type=MESH,
        )

    for p in range(patches):
        wm[p] = jnp.where(tap < pt_ref[p][:, 2:3], w_ref[p].astype(F32), 0.0)
    share_of_steps([0])

    pl.semaphore_wait(barrier, n_patch + n_slab - 2)
    hist_copies = [hist_copy(0, off) for off in range(1, n_slab)]
    for copy in hist_copies:
        copy.start()

    share_of_steps(list(range(1, STEPS)))
    for step in range(1, STEPS):
        for off in range(1, n_slab):
            copy = hist_copy(step, off)
            copy.start()
            hist_copies.append(copy)

    mine = pl.ds(pl.multiple_of(slab * loc, loc), loc)
    table = pt_ref[:, mine, :].reshape(rows, 3)
    weights = wm[:, mine, :].reshape(rows, WMAX)
    for d in range(1, STEPS):
        acc = jnp.zeros((rows, 1), F32)
        for j in range(min(WMAX, d)):
            acc = jnp.where(table[:, 1:2] == d - j, weights[:, j : j + 1], acc)
        recent_w[d] = jnp.broadcast_to(acc, (rows, src))
    target = lax.broadcasted_iota(jnp.int32, (rows, total), 1)
    onehot[...] = (target == table[:, 0:1]).astype(F32).T.astype(BF16)
    for step in range(STEPS):
        inc[step] = inc_ref[:, step, :]

    def repeat(a):
        return jnp.broadcast_to(a[:, None, :], (patches, loc, src)).reshape(rows, src)

    def prepare(step):
        for off in range(1, n_slab):
            hist_copies[step * (n_slab - 1) + off - 1].wait_recv()
        acc = hsend[step, slab].astype(F32)
        for off in range(1, n_slab):
            acc = acc + hrecv[step, off].astype(F32)
        for d in range(2, step + 1):
            acc = acc + recent_w[d] * repeat(amps[step - d])
        pre[...] = acc

    prepare(0)
    for load in loads:
        load.wait()

    remote = []
    for step in range(STEPS):
        driven = pre[...]
        if step > 0:
            driven = driven + recent_w[1] * repeat(amps[step - 1])
        pre[...] = driven

        def couple(p, carry):
            at = pl.ds(pl.multiple_of(p * loc, loc), loc)
            coupled[at, :] = own_blocks(pre[at, :], coup[p])
            return carry

        lax.fori_loop(0, patches, couple, 0, unroll=True)
        whole = coupled[...]
        high = whole.astype(BF16)
        low = (whole - high.astype(F32)).astype(BF16)
        field = jnp.dot(onehot[...], high, preferred_element_type=F32) + jnp.dot(
            onehot[...], low, preferred_element_type=F32
        )
        fsend[step] = field.astype(BF16).reshape(n_patch, patches, src)
        copies = [field_copy(step, off) for off in range(1, n_patch)]
        for copy in copies:
            copy.start()
        for copy in copies:
            copy.wait_recv()
        remote += copies
        share = fsend[step, me].astype(F32)
        for off in range(1, n_patch):
            share = share + frecv[step, off].astype(F32)
        zbuf[step, 0] = share.astype(BF16)
        copies = [slab_copy(step, off) for off in range(1, n_slab)]
        for copy in copies:
            copy.start()
        if step + 1 < STEPS:
            prepare(step + 1)
        for copy in copies:
            copy.wait_recv()
        remote += copies
        scattered = zbuf[step, lax.rem(slab, n_slab)].astype(F32)
        for t in range(1, n_slab):
            scattered = scattered + zbuf[step, lax.rem(slab + n_slab - t, n_slab)].astype(F32)
        drive = inc[step] - scattered
        half = inv.shape[1] // src
        amp = jnp.concatenate(
            [own_blocks(drive[g * half : (g + 1) * half], inv[g]) for g in range(patches // half)],
            axis=0,
        ).astype(BF16)
        out_ref[step] = amp
        amps[step] = amp.astype(F32)

    for copy in hist_copies:
        copy.wait_send()
    for copy in remote:
        copy.wait_send()


def on_device(n_patch, n_slab, history, interp_weights, pair_table, coupling, self_inverse, incident):
    patches, slab_len, src = history.shape
    pairs = pair_table.shape[1]
    loc = coupling.shape[1]
    rows = patches * loc
    total = n_patch * patches
    group = 8
    vmem = pl.BlockSpec(memory_space=pltpu.VMEM)
    hbm = pl.BlockSpec(memory_space=pl.ANY)
    dma = pltpu.SemaphoreType.DMA
    out = pl.pallas_call(
        functools.partial(march, n_patch, n_slab),
        out_shape=jax.ShapeDtypeStruct((STEPS, patches, src), BF16),
        in_specs=[vmem, vmem, vmem, hbm, hbm, vmem],
        out_specs=vmem,
        scratch_shapes=[
            pltpu.VMEM((patches, loc * src, src), BF16),
            pltpu.VMEM((patches // group, group * src, src), BF16),
            pltpu.VMEM((patches, pairs, WMAX), F32),
            pltpu.VMEM((STEPS, rows, src), F32),
            pltpu.VMEM((total, rows), BF16),
            pltpu.VMEM((STEPS, patches, src), F32),
            pltpu.VMEM((STEPS, patches, src), F32),
            pltpu.VMEM((rows, src), F32),
            pltpu.VMEM((rows, src), F32),
            pltpu.VMEM((STEPS, n_slab, rows, src), BF16),
            pltpu.VMEM((STEPS, n_slab, rows, src), BF16),
            pltpu.VMEM((STEPS, n_patch, patches, src), BF16),
            pltpu.VMEM((STEPS, n_patch, patches, src), BF16),
            pltpu.VMEM((STEPS, n_slab, patches, src), BF16),
            dma((5,)),
            dma((STEPS, n_slab)),
            dma((STEPS, n_slab)),
            dma((STEPS, n_patch)),
            dma((STEPS, n_patch)),
            dma((STEPS, n_slab)),
            dma((STEPS, n_slab)),
        ],
        compiler_params=pltpu.CompilerParams(
            collective_id=0, has_side_effects=True, vmem_limit_bytes=40 * 1024 * 1024
        ),
    )(
        history,
        interp_weights,
        pair_table,
        coupling.reshape(patches, loc * src, src),
        self_inverse.reshape(patches // group, group * src, src),
        incident,
    )
    return out.transpose(1, 0, 2)


def solution(mesh):
    in_specs = (
        P("patch", "slab", None),
        P("patch", None, None),
        P("patch", None, None),
        P("patch", "slab", None, None),
        P("patch", None, None),
        P("patch", None, None),
    )
    out_specs = P("patch", None, None)
    return jax.shard_map(
        functools.partial(on_device, mesh.shape["patch"], mesh.shape["slab"]),
        mesh=mesh,
        in_specs=in_specs,
        out_specs=out_specs,
        check_vma=False,
    )
```

time: 273 us -> 53 us (0.19)
  waiting for transfers between devices: 173 us -> 0 us
  blocking collectives: 48 us -> 0 us
  Pallas kernels: 0 us -> 45.2 us
  matrix products: 31.2 us -> 0 us
  between operations: 13.7 us -> 0.02 us
  local copies, waits for them, and re-layouts: 3.27 us -> 7.37 us
  other arithmetic: 2.94 us -> 0 us
    reduce_scatter x8 -> x0, waiting for transfers between devices: 173 us -> none  [the longest x4 123 us: on_device(): lax.psum_scatter(jnp.dot(field_onehot, contrib, precision=lax.Precision.H...]
    psum x4 -> x0, blocking collectives: 48 us -> none  [on_device(): scattered = lax.psum(field_share, 'slab')]
    pallas_call x0 -> x1, Pallas kernels: none -> 45.2 us  [on_device(): pl.pallas_call(functools.partial(march, n_patch, n_slab), out_shape=jax.S...]
    dot_general x20 -> x0, matrix products: 31.2 us -> none  [the longest x4 17.7 us: on_device(): jnp.einsum('pkij,kpj->pki', coupling, driven, preferred_element_type=jnp....]
    unnamed x9 -> x10, local copies, waits for them, and re-layouts: 0.09 us -> 6.76 us
  transfers between devices with their start and end apart: 8 -> 0, of which waited for: 8 -> 0; matrix products, arithmetic and copies ran while one was open for 2% -> 0% of each run, Pallas kernels for 0% -> 0%
where the time goes in v1:
time: 53 us; the launch traced here: 52.6 us
  Pallas kernels  45.2 us (85%)
  local copies, waits for them, and re-layouts  7.37 us (14%)
    pallas_call x1, Pallas kernels, on_device(): pl.pallas_call(functools.partial(march, n_patch, n_slab), out_shape=jax.S...  45.2 us
    unnamed x10, local copies, waits for them, and re-layouts  6.76 us

profile of v1, /device:TPU:0, one launch (start us, length us, event | category | flops | bytes accessed | tf_op | source)
XLA Modules:
  0.0 52.6 jit_solution(14736732540923347179)
XLA Ops:
  0.0 0.9 %copy.7.w_ref = bf16[16,32,4]{2,1,0:T(8,128)(2,1)S(1)} copy(bf16[16,32,4]{1,2,0:T(4,128)(2,1)} %param.7) | data formatting | bytes 8192 | tf_op args[1]
  0.9 0.9 %copy.8.pt_ref = s32[16,32,3]{2,1,0:T(8,128)S(1)} copy(s32[16,32,3]{1,0,2:T(8,128)} %param.8) | data formatting | bytes 12288 | tf_op args[2]
  1.8 0.0 copy-start
  1.8 2.2 %copy-done = bf16[16,8,128,128]{3,2,1,0:T(8,128)(2,1)S(1)} copy-done((bf16[16,8,128,128]{3,2,1,0:T(8,128)(2,1)S(1)}, bf16[16,8,128,128]{3,2,1,0:T(8,128)(2,1)}, u32[]{:S(2)}) %copy-start) | copy-done | bytes 4194328
  4.0 0.0 copy-start.1
  4.0 1.0 %copy-done.1 = bf16[16,128,128]{2,1,0:T(8,128)(2,1)S(1)} copy-done((bf16[16,128,128]{2,1,0:T(8,128)(2,1)S(1)}, bf16[16,128,128]{2,1,0:T(8,128)(2,1)}, u32[]{:S(2)}) %copy-start.1) | copy-done | bytes 524312
  5.1 0.0 copy-start.2
  5.1 0.9 %copy-done.2 = bf16[16,64,128]{2,1,0:T(8,128)(2,1)S(1)} copy-done((bf16[16,64,128]{2,1,0:T(8,128)(2,1)S(1)}, bf16[16,64,128]{2,1,0:T(8,128)(2,1)}, u32[]{:S(2)}) %copy-start.2) | copy-done | bytes 262168
  6.0 0.0 copy-start.3
  6.0 0.8 %copy-done.3 = f32[16,4,128]{2,1,0:T(4,128)S(1)} copy-done((f32[16,4,128]{2,1,0:T(4,128)S(1)}, f32[16,4,128]{2,1,0:T(4,128)}, u32[]{:S(2)}) %copy-start.3) | copy-done | bytes 32792
  6.8 45.2 %shard_map.64 = bf16[4,16,128]{2,1,0:T(8,128)(2,1)S(1)} custom-call(bf16[16,64,128]{2,1,0:T(8,128)(2,1)S(1)} %copy-done.2, bf16[16,32,4]{2,1,0:T(8,128)(2,1)S(1)} %copy.7.w_ref, s32[16,32,3]{2,1,0:T(8,128)S(1)} %copy.8.pt_ref, bf16[16,1024,128]{2,1,0:T(8,128)(2,1)S(1)} %bitcast.3, bf16[2,1024,128]{2,1,0:T(8,128)(2,1)S(1)} %bitcast.4, f32[16,4,128]{2,1,0:T(4,128)S(1)} %copy-done.3), custom_call_target="tpu_custom_call" | custom-call | tf_op jit(solution)/shard_map/pallas_call | solution.py:273
  51.9 0.6 %copy.9 = bf16[16,4,128]{2,1,0:T(4,128)(2,1)} copy(bf16[16,4,128]{2,0,1:T(8,128)(2,1)S(1)} %bitcast.5) | data formatting | bytes 32768 | tf_op jit(solution)/shard_map/transpose | solution.py:312
Async XLA Ops:
  1.8 2.2 %copy-start = (bf16[16,8,128,128]{3,2,1,0:T(8,128)(2,1)S(1)}, bf16[16,8,128,128]{3,2,1,0:T(8,128)(2,1)}, u32[]{:S(2)}) copy-start(bf16[16,8,128,128]{3,2,1,0:T(8,128)(2,1)} %param.9) | copy-start | bytes 12582916
  4.0 1.0 %copy-start.1 = (bf16[16,128,128]{2,1,0:T(8,128)(2,1)S(1)}, bf16[16,128,128]{2,1,0:T(8,128)(2,1)}, u32[]{:S(2)}) copy-start(bf16[16,128,128]{2,1,0:T(8,128)(2,1)} %param.10) | copy-start | bytes 1572868
  5.1 0.9 %copy-start.2 = (bf16[16,64,128]{2,1,0:T(8,128)(2,1)S(1)}, bf16[16,64,128]{2,1,0:T(8,128)(2,1)}, u32[]{:S(2)}) copy-start(bf16[16,64,128]{2,1,0:T(8,128)(2,1)} %hist_ref.1) | copy-start | bytes 786436
  6.0 0.8 %copy-start.3 = (f32[16,4,128]{2,1,0:T(4,128)S(1)}, f32[16,4,128]{2,1,0:T(4,128)}, u32[]{:S(2)}) copy-start(f32[16,4,128]{2,1,0:T(4,128)} %inc_ref.1) | copy-start | bytes 98308

commit v2 on v1

--- a/solution.py
+++ b/solution.py
@@ -31,15 +31,21 @@
 def march(
     n_patch,
     n_slab,
+    hist_hbm,
+    w_hbm,
+    pt_hbm,
+    coup_hbm,
+    inv_hbm,
+    inc_hbm,
+    out_ref,
     hist_ref,
     w_ref,
     pt_ref,
-    coup_hbm,
-    inv_hbm,
     inc_ref,
-    out_ref,
     coup,
     inv,
+    first_t,
+    obs_t,
     wm,
     recent_w,
     onehot,
@@ -61,7 +67,7 @@
     z_recv_sem,
 ):
     patches, slab_len, src = hist_ref.shape
-    pairs = pt_ref.shape[1]
+    pairs = pt_ref.shape[2]
     loc = pairs // n_slab
     rows = patches * loc
     total = n_patch * patches
@@ -74,6 +80,14 @@
     def slab_peer(off):
         return lax.rem(slab + off, n_slab)
 
+    small = [(pt_hbm, pt_ref), (w_hbm, w_ref), (hist_hbm, hist_ref), (inc_hbm, inc_ref)]
+    small = [
+        pltpu.make_async_copy(src_hbm, dst, local_sem.at[c])
+        for c, (src_hbm, dst) in enumerate(small)
+    ]
+    for load in small:
+        load.start()
+
     barrier = pltpu.get_barrier_semaphore()
     for off in range(1, n_patch):
         pl.semaphore_signal(
@@ -88,43 +102,39 @@
     size = patches // parts
     loads = [
         pltpu.make_async_copy(
-            coup_hbm.at[pl.ds(c * size, size)], coup.at[pl.ds(c * size, size)], local_sem.at[c]
+            coup_hbm.at[pl.ds(c * size, size)],
+            coup.at[pl.ds(c * size, size)],
+            local_sem.at[len(small) + c],
         )
         for c in range(parts)
     ]
-    loads.append(pltpu.make_async_copy(inv_hbm, inv, local_sem.at[parts]))
+    loads.append(pltpu.make_async_copy(inv_hbm, inv, local_sem.at[len(small) + parts]))
     for load in loads:
         load.start()
 
     lane = lax.broadcasted_iota(jnp.int32, (pairs, slab_len), 1) + (slab * slab_len + 1)
-    tap = lax.broadcasted_iota(jnp.int32, (pairs, WMAX), 1)
 
     def stored_share(p, steps):
-        table = pt_ref[p]
-        weights = wm[p]
-        shift = lane - table[:, 1:2]
+        shift = lane - first_t[:, p : p + 1]
+        taps = [wm[j, :, p : p + 1] for j in range(WMAX)]
         hits = []
         for step in steps:
             hit = jnp.zeros((pairs, slab_len), F32)
             for j in range(WMAX):
-                hit = jnp.where(shift == j - step, weights[:, j : j + 1], hit)
+                hit = jnp.where(shift == j - step, taps[j], hit)
             hits.append(hit)
         hit = hits[0] if len(hits) == 1 else jnp.concatenate(hits, axis=0)
         return jnp.dot(hit.astype(BF16), hist_ref[p], preferred_element_type=F32)
 
     def share_of_steps(steps):
-        def two(i, carry):
-            a = stored_share(2 * i, steps)
-            b = stored_share(2 * i + 1, steps)
-            at = pl.ds(pl.multiple_of(i * 2 * loc, 2 * loc), 2 * loc)
+        for i in range(0, patches, 2):
+            a = stored_share(i, steps)
+            b = stored_share(i + 1, steps)
             for k, step in enumerate(steps):
                 for d in range(n_slab):
                     r = k * pairs + d * loc
                     both = jnp.concatenate([a[r : r + loc], b[r : r + loc]], axis=0)
-                    hsend[step, d, at, :] = both.astype(BF16)
-            return carry
-
-        lax.fori_loop(0, patches // 2, two, 0, unroll=True)
+                    hsend[step, d, i * loc : (i + 2) * loc, :] = both.astype(BF16)
 
     def hist_copy(step, off):
         dest = slab_peer(off)
@@ -158,32 +168,45 @@
             device_id_type=MESH,
         )
 
-    for p in range(patches):
-        wm[p] = jnp.where(tap < pt_ref[p][:, 2:3], w_ref[p].astype(F32), 0.0)
+    small[0].wait()
+    small[1].wait()
+    obs_t[...] = pt_ref[0].T
+    first_t[...] = pt_ref[1].T
+    band_t = pt_ref[2].T
+    weights = w_ref[...].astype(F32)
+    for j in range(WMAX):
+        wm[j] = jnp.where(j < band_t, weights[:, j, :].T, 0.0)
+    small[2].wait()
+    small[3].wait()
     share_of_steps([0])
 
     pl.semaphore_wait(barrier, n_patch + n_slab - 2)
-    hist_copies = [hist_copy(0, off) for off in range(1, n_slab)]
-    for copy in hist_copies:
-        copy.start()
-
-    share_of_steps(list(range(1, STEPS)))
-    for step in range(1, STEPS):
+    hist_copies = []
+
+    def send_hist(step):
         for off in range(1, n_slab):
             copy = hist_copy(step, off)
             copy.start()
             hist_copies.append(copy)
 
+    send_hist(0)
+    share_of_steps(list(range(1, STEPS)))
+    send_hist(1)
+
     mine = pl.ds(pl.multiple_of(slab * loc, loc), loc)
-    table = pt_ref[:, mine, :].reshape(rows, 3)
-    weights = wm[:, mine, :].reshape(rows, WMAX)
+
+    def column(x):
+        return jnp.concatenate([x[:, p : p + 1] for p in range(patches)], axis=0)
+
+    first = column(first_t[mine, :])
+    taps = [column(wm[j, mine, :]) for j in range(min(WMAX, STEPS - 1))]
     for d in range(1, STEPS):
         acc = jnp.zeros((rows, 1), F32)
         for j in range(min(WMAX, d)):
-            acc = jnp.where(table[:, 1:2] == d - j, weights[:, j : j + 1], acc)
+            acc = jnp.where(first == d - j, taps[j], acc)
         recent_w[d] = jnp.broadcast_to(acc, (rows, src))
     target = lax.broadcasted_iota(jnp.int32, (rows, total), 1)
-    onehot[...] = (target == table[:, 0:1]).astype(F32).T.astype(BF16)
+    onehot[...] = (target == column(obs_t[mine, :])).astype(F32).T.astype(BF16)
     for step in range(STEPS):
         inc[step] = inc_ref[:, step, :]
 
@@ -242,6 +265,8 @@
         for copy in copies:
             copy.wait_recv()
         remote += copies
+        if step + 2 < STEPS:
+            send_hist(step + 2)
         scattered = zbuf[step, lax.rem(slab, n_slab)].astype(F32)
         for t in range(1, n_slab):
             scattered = scattered + zbuf[step, lax.rem(slab + n_slab - t, n_slab)].astype(F32)
@@ -268,17 +293,23 @@
     total = n_patch * patches
     group = 8
     vmem = pl.BlockSpec(memory_space=pltpu.VMEM)
-    hbm = pl.BlockSpec(memory_space=pl.ANY)
+    hbm = pl.BlockSpec(memory_space=pltpu.HBM)
     dma = pltpu.SemaphoreType.DMA
     out = pl.pallas_call(
         functools.partial(march, n_patch, n_slab),
         out_shape=jax.ShapeDtypeStruct((STEPS, patches, src), BF16),
-        in_specs=[vmem, vmem, vmem, hbm, hbm, vmem],
+        in_specs=[hbm] * 6,
         out_specs=vmem,
         scratch_shapes=[
+            pltpu.VMEM((patches, slab_len, src), BF16),
+            pltpu.VMEM((patches, WMAX, pairs), BF16),
+            pltpu.VMEM((3, patches, pairs), jnp.int32),
+            pltpu.VMEM((patches, STEPS, src), F32),
             pltpu.VMEM((patches, loc * src, src), BF16),
             pltpu.VMEM((patches // group, group * src, src), BF16),
-            pltpu.VMEM((patches, pairs, WMAX), F32),
+            pltpu.VMEM((pairs, patches), jnp.int32),
+            pltpu.VMEM((pairs, patches), jnp.int32),
+            pltpu.VMEM((WMAX, pairs, patches), F32),
             pltpu.VMEM((STEPS, rows, src), F32),
             pltpu.VMEM((total, rows), BF16),
             pltpu.VMEM((STEPS, patches, src), F32),
@@ -290,7 +321,7 @@
             pltpu.VMEM((STEPS, n_patch, patches, src), BF16),
             pltpu.VMEM((STEPS, n_patch, patches, src), BF16),
             pltpu.VMEM((STEPS, n_slab, patches, src), BF16),
-            dma((5,)),
+            dma((9,)),
             dma((STEPS, n_slab)),
             dma((STEPS, n_slab)),
             dma((STEPS, n_patch)),
@@ -299,12 +330,12 @@
             dma((STEPS, n_slab)),
         ],
         compiler_params=pltpu.CompilerParams(
-            collective_id=0, has_side_effects=True, vmem_limit_bytes=40 * 1024 * 1024
+            collective_id=0, has_side_effects=True, vmem_limit_bytes=63 * 1024 * 1024
         ),
     )(
         history,
-        interp_weights,
-        pair_table,
+        interp_weights.transpose(0, 2, 1),
+        pair_table.transpose(2, 0, 1),
         coupling.reshape(patches, loc * src, src),
         self_inverse.reshape(patches // group, group * src, src),
         incident,

time: 53 us -> 47.3 us (0.89)
  local copies, waits for them, and re-layouts: 7.37 us -> 1.33 us
  Pallas kernels: 45.2 us -> 45.8 us
    unnamed x10 -> x0, local copies, waits for them, and re-layouts: 6.76 us -> none
    transpose x1, local copies, waits for them, and re-layouts: 0.61 us -> 1.33 us  [on_device(): return out.transpose(1, 0, 2)]
    pallas_call x1, Pallas kernels: 45.2 us -> 45.8 us  [on_device(): pl.pallas_call(functools.partial(march, n_patch, n_slab), out_shape=jax.S...]
where the time goes in v2:
time: 47.3 us; the launch traced here: 47.1 us
  Pallas kernels  45.8 us (97%)
  local copies, waits for them, and re-layouts  1.33 us (3%)
    pallas_call x1, Pallas kernels, on_device(): pl.pallas_call(functools.partial(march, n_patch, n_slab), out_shape=jax.S...  45.8 us
    transpose x1, local copies, waits for them, and re-layouts, on_device(): return out.transpose(1, 0, 2)  1.33 us

profile of v2, /device:TPU:0, one launch (start us, length us, event | category | flops | bytes accessed | tf_op | source)
XLA Modules:
  0.0 47.1 jit_solution(9187882465430214248)
XLA Ops:
  0.0 45.8 %shard_map.64 = bf16[4,16,128]{2,1,0:T(8,128)(2,1)} custom-call(bf16[16,64,128]{2,1,0:T(8,128)(2,1)} %hist_hbm.1, bf16[16,4,32]{2,1,0:T(4,128)(2,1)} %bitcast.9, s32[3,16,32]{2,1,0:T(8,128)} %bitcast.8, bf16[16,1024,128]{2,1,0:T(8,128)(2,1)} %bitcast.5, bf16[2,1024,128]{2,1,0:T(8,128)(2,1)} %bitcast.6, f32[16,4,128]{2,1,0:T(4,128)} %inc_hbm.1), custom_call_target="tpu_custom_call" | custom-call | tf_op jit(solution)/shard_map/pallas_call | solution.py:298
  45.8 1.3 %copy.7 = bf16[16,4,128]{2,1,0:T(4,128)(2,1)} copy(bf16[16,4,128]{2,0,1:T(8,128)(2,1)} %bitcast.7) | data formatting | bytes 32768 | tf_op jit(solution)/shard_map/transpose | solution.py:343

commit v3 on v2

--- a/solution.py
+++ b/solution.py
@@ -14,16 +14,17 @@
 BF16 = jnp.bfloat16
 
 
-def nt_dot(x, m):
-    return lax.dot_general(x, m, (((1,), (1,)), ((), ())), preferred_element_type=F32)
-
-
 def own_blocks(x, m):
     rows, src = x.shape
-    full = nt_dot(x.astype(BF16), m)
-    row = lax.broadcasted_iota(jnp.int32, (rows, src), 0)
+    half = rows // 2
+    wide = jnp.concatenate([x, x], axis=1)
+    row = lax.broadcasted_iota(jnp.int32, wide.shape, 0)
+    lane = lax.broadcasted_iota(jnp.int32, wide.shape, 1)
+    wide = jnp.where((row < half) == (lane < src), wide, 0.0).astype(BF16)
+    full = jnp.dot(wide, m, preferred_element_type=F32)
+    row = lax.rem(lax.broadcasted_iota(jnp.int32, (rows, src), 0), half)
     out = full[:, :src]
-    for r in range(1, rows):
+    for r in range(1, half):
         out = jnp.where(row == r, full[:, r * src : (r + 1) * src], out)
     return out
 
@@ -44,6 +45,8 @@
     inc_ref,
     coup,
     inv,
+    coup_t,
+    inv_t,
     first_t,
     obs_t,
     wm,
@@ -223,9 +226,20 @@
             acc = acc + recent_w[d] * repeat(amps[step - d])
         pre[...] = acc
 
-    prepare(0)
     for load in loads:
         load.wait()
+
+    def turn(stored, turned):
+        pairs_of, _, width = turned.shape
+        for g in range(pairs_of):
+            for h in range(2):
+                for r in range(width // src):
+                    block = stored[2 * g + h, r * src : (r + 1) * src, :]
+                    turned[g, h * src : (h + 1) * src, r * src : (r + 1) * src] = block.T
+
+    turn(coup, coup_t)
+    turn(inv, inv_t)
+    prepare(0)
 
     remote = []
     for step in range(STEPS):
@@ -235,11 +249,11 @@
         pre[...] = driven
 
         def couple(p, carry):
-            at = pl.ds(pl.multiple_of(p * loc, loc), loc)
-            coupled[at, :] = own_blocks(pre[at, :], coup[p])
+            at = pl.ds(pl.multiple_of(p * 2 * loc, 2 * loc), 2 * loc)
+            coupled[at, :] = own_blocks(pre[at, :], coup_t[p])
             return carry
 
-        lax.fori_loop(0, patches, couple, 0, unroll=True)
+        lax.fori_loop(0, patches // 2, couple, 0, unroll=True)
         whole = coupled[...]
         high = whole.astype(BF16)
         low = (whole - high.astype(F32)).astype(BF16)
@@ -271,11 +285,7 @@
         for t in range(1, n_slab):
             scattered = scattered + zbuf[step, lax.rem(slab + n_slab - t, n_slab)].astype(F32)
         drive = inc[step] - scattered
-        half = inv.shape[1] // src
-        amp = jnp.concatenate(
-            [own_blocks(drive[g * half : (g + 1) * half], inv[g]) for g in range(patches // half)],
-            axis=0,
-        ).astype(BF16)
+        amp = own_blocks(drive, inv_t[0]).astype(BF16)
         out_ref[step] = amp
         amps[step] = amp.astype(F32)
 
@@ -291,7 +301,7 @@
     loc = coupling.shape[1]
     rows = patches * loc
     total = n_patch * patches
-    group = 8
+    group = patches // 2
     vmem = pl.BlockSpec(memory_space=pltpu.VMEM)
     hbm = pl.BlockSpec(memory_space=pltpu.HBM)
     dma = pltpu.SemaphoreType.DMA
@@ -307,6 +317,8 @@
             pltpu.VMEM((patches, STEPS, src), F32),
             pltpu.VMEM((patches, loc * src, src), BF16),
             pltpu.VMEM((patches // group, group * src, src), BF16),
+            pltpu.VMEM((patches // 2, 2 * src, loc * src), BF16),
+            pltpu.VMEM((1, 2 * src, group * src), BF16),
             pltpu.VMEM((pairs, patches), jnp.int32),
             pltpu.VMEM((pairs, patches), jnp.int32),
             pltpu.VMEM((WMAX, pairs, patches), F32),

time: 47.3 us -> 44.9 us (0.949)
  Pallas kernels: 45.8 us -> 43.3 us
    pallas_call x1, Pallas kernels: 45.8 us -> 43.3 us  [on_device(): pl.pallas_call(functools.partial(march, n_patch, n_slab), out_shape=jax.S...]
where the time goes in v3:
time: 44.9 us; the launch traced here: 44.7 us
  Pallas kernels  43.3 us (96%)
  local copies, waits for them, and re-layouts  1.33 us (3%)
    pallas_call x1, Pallas kernels, on_device(): pl.pallas_call(functools.partial(march, n_patch, n_slab), out_shape=jax.S...  43.3 us
    transpose x1, local copies, waits for them, and re-layouts, on_device(): return out.transpose(1, 0, 2)  1.33 us

profile of v3, /device:TPU:0, one launch (start us, length us, event | category | flops | bytes accessed | tf_op | source)
XLA Modules:
  0.0 44.7 jit_solution(10723053709224212097)
XLA Ops:
  0.0 43.3 %shard_map.64 = bf16[4,16,128]{2,1,0:T(8,128)(2,1)} custom-call(bf16[16,64,128]{2,1,0:T(8,128)(2,1)} %hist_hbm.1, bf16[16,4,32]{2,1,0:T(4,128)(2,1)} %bitcast.9, s32[3,16,32]{2,1,0:T(8,128)} %bitcast.8, bf16[16,1024,128]{2,1,0:T(8,128)(2,1)} %bitcast.5, bf16[2,1024,128]{2,1,0:T(8,128)(2,1)} %bitcast.6, f32[16,4,128]{2,1,0:T(4,128)} %inc_hbm.1), custom_call_target="tpu_custom_call" | custom-call | tf_op jit(solution)/shard_map/pallas_call | solution.py:308
  43.3 1.3 %copy.7 = bf16[16,4,128]{2,1,0:T(4,128)(2,1)} copy(bf16[16,4,128]{2,0,1:T(8,128)(2,1)} %bitcast.7) | data formatting | bytes 32768 | tf_op jit(solution)/shard_map/transpose | solution.py:355

commit v4 on v3

--- a/solution.py
+++ b/solution.py
@@ -144,8 +144,8 @@
         return pltpu.make_async_remote_copy(
             src_ref=hsend.at[step, dest],
             dst_ref=hrecv.at[step, off],
-            send_sem=h_send_sem.at[step, off],
-            recv_sem=h_recv_sem.at[step, off],
+            send_sem=h_send_sem.at[step],
+            recv_sem=h_recv_sem.at[step],
             device_id={"patch": me, "slab": dest},
             device_id_type=MESH,
         )
@@ -155,8 +155,8 @@
         return pltpu.make_async_remote_copy(
             src_ref=fsend.at[step, dest],
             dst_ref=frecv.at[step, off],
-            send_sem=f_send_sem.at[step, off],
-            recv_sem=f_recv_sem.at[step, off],
+            send_sem=f_send_sem.at[step],
+            recv_sem=f_recv_sem.at[step],
             device_id={"patch": dest, "slab": slab},
             device_id_type=MESH,
         )
@@ -165,9 +165,20 @@
         return pltpu.make_async_remote_copy(
             src_ref=zbuf.at[step, 0],
             dst_ref=zbuf.at[step, off],
-            send_sem=z_send_sem.at[step, off],
-            recv_sem=z_recv_sem.at[step, off],
+            send_sem=z_send_sem.at[step],
+            recv_sem=z_recv_sem.at[step],
             device_id={"patch": me, "slab": slab_peer(off)},
+            device_id_type=MESH,
+        )
+
+    def all_of(step, ref, send_sem, recv_sem):
+        slots = ref.at[step, pl.ds(1, ref.shape[1] - 1)]
+        return pltpu.make_async_remote_copy(
+            src_ref=slots,
+            dst_ref=slots,
+            send_sem=send_sem.at[step],
+            recv_sem=recv_sem.at[step],
+            device_id={"patch": me, "slab": slab_peer(1)},
             device_id_type=MESH,
         )
 
@@ -184,16 +195,13 @@
     share_of_steps([0])
 
     pl.semaphore_wait(barrier, n_patch + n_slab - 2)
-    hist_copies = []
 
     def send_hist(step):
-        for off in range(1, n_slab):
-            copy = hist_copy(step, off)
-            copy.start()
-            hist_copies.append(copy)
+        for off in range(n_slab - 1, 0, -1):
+            hist_copy(step, off).start()
 
     send_hist(0)
-    share_of_steps(list(range(1, STEPS)))
+    share_of_steps([1])
     send_hist(1)
 
     mine = pl.ds(pl.multiple_of(slab * loc, loc), loc)
@@ -217,8 +225,7 @@
         return jnp.broadcast_to(a[:, None, :], (patches, loc, src)).reshape(rows, src)
 
     def prepare(step):
-        for off in range(1, n_slab):
-            hist_copies[step * (n_slab - 1) + off - 1].wait_recv()
+        all_of(step, hrecv, h_send_sem, h_recv_sem).wait_recv()
         acc = hsend[step, slab].astype(F32)
         for off in range(1, n_slab):
             acc = acc + hrecv[step, off].astype(F32)
@@ -241,7 +248,6 @@
     turn(inv, inv_t)
     prepare(0)
 
-    remote = []
     for step in range(STEPS):
         driven = pre[...]
         if step > 0:
@@ -261,24 +267,20 @@
             onehot[...], low, preferred_element_type=F32
         )
         fsend[step] = field.astype(BF16).reshape(n_patch, patches, src)
-        copies = [field_copy(step, off) for off in range(1, n_patch)]
-        for copy in copies:
-            copy.start()
-        for copy in copies:
-            copy.wait_recv()
-        remote += copies
+        for off in range(n_patch - 1, 0, -1):
+            field_copy(step, off).start()
+        if step == 0:
+            share_of_steps(list(range(2, STEPS)))
+        all_of(step, frecv, f_send_sem, f_recv_sem).wait_recv()
         share = fsend[step, me].astype(F32)
         for off in range(1, n_patch):
             share = share + frecv[step, off].astype(F32)
         zbuf[step, 0] = share.astype(BF16)
-        copies = [slab_copy(step, off) for off in range(1, n_slab)]
-        for copy in copies:
-            copy.start()
+        for off in range(n_slab - 1, 0, -1):
+            slab_copy(step, off).start()
         if step + 1 < STEPS:
             prepare(step + 1)
-        for copy in copies:
-            copy.wait_recv()
-        remote += copies
+        all_of(step, zbuf, z_send_sem, z_recv_sem).wait_recv()
         if step + 2 < STEPS:
             send_hist(step + 2)
         scattered = zbuf[step, lax.rem(slab, n_slab)].astype(F32)
@@ -289,10 +291,10 @@
         out_ref[step] = amp
         amps[step] = amp.astype(F32)
 
-    for copy in hist_copies:
-        copy.wait_send()
-    for copy in remote:
-        copy.wait_send()
+    for step in range(STEPS):
+        all_of(step, hsend, h_send_sem, h_recv_sem).wait_send()
+        all_of(step, fsend, f_send_sem, f_recv_sem).wait_send()
+        all_of(step, zbuf, z_send_sem, z_recv_sem).wait_send()
 
 
 def on_device(n_patch, n_slab, history, interp_weights, pair_table, coupling, self_inverse, incident):
@@ -334,12 +336,12 @@
             pltpu.VMEM((STEPS, n_patch, patches, src), BF16),
             pltpu.VMEM((STEPS, n_slab, patches, src), BF16),
             dma((9,)),
-            dma((STEPS, n_slab)),
-            dma((STEPS, n_slab)),
-            dma((STEPS, n_patch)),
-            dma((STEPS, n_patch)),
-            dma((STEPS, n_slab)),
-            dma((STEPS, n_slab)),
+            dma((STEPS,)),
+            dma((STEPS,)),
+            dma((STEPS,)),
+            dma((STEPS,)),
+            dma((STEPS,)),
+            dma((STEPS,)),
         ],
         compiler_params=pltpu.CompilerParams(
             collective_id=0, has_side_effects=True, vmem_limit_bytes=63 * 1024 * 1024

time: 44.9 us -> 44.2 us (0.984)
  Pallas kernels: 43.3 us -> 42.6 us
    pallas_call x1, Pallas kernels: 43.3 us -> 42.6 us  [on_device(): pl.pallas_call(functools.partial(march, n_patch, n_slab), out_shape=jax.S...]
where the time goes in v4:
time: 44.2 us; the launch traced here: 44 us
  Pallas kernels  42.6 us (96%)
  local copies, waits for them, and re-layouts  1.33 us (3%)
    pallas_call x1, Pallas kernels, on_device(): pl.pallas_call(functools.partial(march, n_patch, n_slab), out_shape=jax.S...  42.6 us
    transpose x1, local copies, waits for them, and re-layouts, on_device(): return out.transpose(1, 0, 2)  1.33 us

profile of v4, /device:TPU:0, one launch (start us, length us, event | category | flops | bytes accessed | tf_op | source)
XLA Modules:
  0.0 44.0 jit_solution(6864146243804788597)
XLA Ops:
  0.0 42.6 %shard_map.64 = bf16[4,16,128]{2,1,0:T(8,128)(2,1)} custom-call(bf16[16,64,128]{2,1,0:T(8,128)(2,1)} %hist_hbm.1, bf16[16,4,32]{2,1,0:T(4,128)(2,1)} %bitcast.9, s32[3,16,32]{2,1,0:T(8,128)} %bitcast.8, bf16[16,1024,128]{2,1,0:T(8,128)(2,1)} %bitcast.5, bf16[2,1024,128]{2,1,0:T(8,128)(2,1)} %bitcast.6, f32[16,4,128]{2,1,0:T(4,128)} %inc_hbm.1), custom_call_target="tpu_custom_call" | custom-call | tf_op jit(solution)/shard_map/pallas_call | solution.py:310
  42.7 1.3 %copy.7 = bf16[16,4,128]{2,1,0:T(4,128)(2,1)} copy(bf16[16,4,128]{2,0,1:T(8,128)(2,1)} %bitcast.7) | data formatting | bytes 32768 | tf_op jit(solution)/shard_map/transpose | solution.py:357

commit v5 on v4

--- a/solution.py
+++ b/solution.py
@@ -14,14 +14,19 @@
 BF16 = jnp.bfloat16
 
 
-def own_blocks(x, m):
+def own_blocks(x, first, second):
     rows, src = x.shape
     half = rows // 2
     wide = jnp.concatenate([x, x], axis=1)
     row = lax.broadcasted_iota(jnp.int32, wide.shape, 0)
     lane = lax.broadcasted_iota(jnp.int32, wide.shape, 1)
     wide = jnp.where((row < half) == (lane < src), wide, 0.0).astype(BF16)
-    full = jnp.dot(wide, m, preferred_element_type=F32)
+    full = lax.dot_general(
+        wide,
+        jnp.concatenate([first, second], axis=1),
+        (((1,), (1,)), ((), ())),
+        preferred_element_type=F32,
+    )
     row = lax.rem(lax.broadcasted_iota(jnp.int32, (rows, src), 0), half)
     out = full[:, :src]
     for r in range(1, half):
@@ -45,8 +50,6 @@
     inc_ref,
     coup,
     inv,
-    coup_t,
-    inv_t,
     first_t,
     obs_t,
     wm,
@@ -217,7 +220,8 @@
             acc = jnp.where(first == d - j, taps[j], acc)
         recent_w[d] = jnp.broadcast_to(acc, (rows, src))
     target = lax.broadcasted_iota(jnp.int32, (rows, total), 1)
-    onehot[...] = (target == column(obs_t[mine, :])).astype(F32).T.astype(BF16)
+    hit = (target == column(obs_t[mine, :])).astype(F32).T.astype(BF16)
+    onehot[...] = jnp.concatenate([hit, hit], axis=1)
     for step in range(STEPS):
         inc[step] = inc_ref[:, step, :]
 
@@ -236,16 +240,6 @@
     for load in loads:
         load.wait()
 
-    def turn(stored, turned):
-        pairs_of, _, width = turned.shape
-        for g in range(pairs_of):
-            for h in range(2):
-                for r in range(width // src):
-                    block = stored[2 * g + h, r * src : (r + 1) * src, :]
-                    turned[g, h * src : (h + 1) * src, r * src : (r + 1) * src] = block.T
-
-    turn(coup, coup_t)
-    turn(inv, inv_t)
     prepare(0)
 
     for step in range(STEPS):
@@ -256,16 +250,15 @@
 
         def couple(p, carry):
             at = pl.ds(pl.multiple_of(p * 2 * loc, 2 * loc), 2 * loc)
-            coupled[at, :] = own_blocks(pre[at, :], coup_t[p])
+            coupled[at, :] = own_blocks(pre[at, :], coup[2 * p], coup[2 * p + 1])
             return carry
 
         lax.fori_loop(0, patches // 2, couple, 0, unroll=True)
         whole = coupled[...]
         high = whole.astype(BF16)
         low = (whole - high.astype(F32)).astype(BF16)
-        field = jnp.dot(onehot[...], high, preferred_element_type=F32) + jnp.dot(
-            onehot[...], low, preferred_element_type=F32
-        )
+        both = jnp.concatenate([high, low], axis=0)
+        field = jnp.dot(onehot[...], both, preferred_element_type=F32)
         fsend[step] = field.astype(BF16).reshape(n_patch, patches, src)
         for off in range(n_patch - 1, 0, -1):
             field_copy(step, off).start()
@@ -287,7 +280,7 @@
         for t in range(1, n_slab):
             scattered = scattered + zbuf[step, lax.rem(slab + n_slab - t, n_slab)].astype(F32)
         drive = inc[step] - scattered
-        amp = own_blocks(drive, inv_t[0]).astype(BF16)
+        amp = own_blocks(drive, inv[0], inv[1]).astype(BF16)
         out_ref[step] = amp
         amps[step] = amp.astype(F32)
 
@@ -309,7 +302,7 @@
     dma = pltpu.SemaphoreType.DMA
     out = pl.pallas_call(
         functools.partial(march, n_patch, n_slab),
-        out_shape=jax.ShapeDtypeStruct((STEPS, patches, src), BF16),
+        out_shape=pltpu.VMEM((STEPS, patches, src), BF16),
         in_specs=[hbm] * 6,
         out_specs=vmem,
         scratch_shapes=[
@@ -319,13 +312,11 @@
             pltpu.VMEM((patches, STEPS, src), F32),
             pltpu.VMEM((patches, loc * src, src), BF16),
             pltpu.VMEM((patches // group, group * src, src), BF16),
-            pltpu.VMEM((patches // 2, 2 * src, loc * src), BF16),
-            pltpu.VMEM((1, 2 * src, group * src), BF16),
             pltpu.VMEM((pairs, patches), jnp.int32),
             pltpu.VMEM((pairs, patches), jnp.int32),
             pltpu.VMEM((WMAX, pairs, patches), F32),
             pltpu.VMEM((STEPS, rows, src), F32),
-            pltpu.VMEM((total, rows), BF16),
+            pltpu.VMEM((total, 2 * rows), BF16),
             pltpu.VMEM((STEPS, patches, src), F32),
             pltpu.VMEM((STEPS, patches, src), F32),
             pltpu.VMEM((rows, src), F32),
@@ -344,7 +335,7 @@
             dma((STEPS,)),
         ],
         compiler_params=pltpu.CompilerParams(
-            collective_id=0, has_side_effects=True, vmem_limit_bytes=63 * 1024 * 1024
+            collective_id=0, has_side_effects=True, vmem_limit_bytes=62 * 1024 * 1024
         ),
     )(
         history,

time: 44.2 us -> 45.2 us (1.023)
  Pallas kernels: 42.6 us -> 44.4 us
  local copies, waits for them, and re-layouts: 1.33 us -> 0.61 us
    pallas_call x1, Pallas kernels: 42.6 us -> 44.4 us  [on_device(): pl.pallas_call(functools.partial(march, n_patch, n_slab), out_shape=pltpu...]
    transpose x1, local copies, waits for them, and re-layouts: 1.33 us -> 0.61 us  [on_device(): return out.transpose(1, 0, 2)]
where the time goes in v5:
time: 45.2 us; the launch traced here: 45 us
  Pallas kernels  44.4 us (98%)
  local copies, waits for them, and re-layouts  0.61 us (1%)
    pallas_call x1, Pallas kernels, on_device(): pl.pallas_call(functools.partial(march, n_patch, n_slab), out_shape=pltpu...  44.4 us

profile of v5, /device:TPU:0, one launch (start us, length us, event | category | flops | bytes accessed | tf_op | source)
XLA Modules:
  0.0 45.0 jit_solution(14263937724825364366)
XLA Ops:
  0.0 44.4 %shard_map.64 = bf16[4,16,128]{2,1,0:T(8,128)(2,1)S(1)} custom-call(bf16[16,64,128]{2,1,0:T(8,128)(2,1)} %hist_hbm.1, bf16[16,4,32]{2,1,0:T(4,128)(2,1)} %bitcast.9, s32[3,16,32]{2,1,0:T(8,128)} %bitcast.8, bf16[16,1024,128]{2,1,0:T(8,128)(2,1)} %bitcast.6, bf16[2,1024,128]{2,1,0:T(8,128)(2,1)} %bitcast.7, f32[16,4,128]{2,1,0:T(4,128)} %inc_hbm.1), custom_call_target="tpu_custom_call" | custom-call | tf_op jit(solution)/shard_map/pallas_call | solution.py:303
  44.4 0.6 %copy.7 = bf16[16,4,128]{2,1,0:T(4,128)(2,1)} copy(bf16[16,4,128]{2,0,1:T(8,128)(2,1)S(1)} %bitcast.5) | data formatting | bytes 32768 | tf_op jit(solution)/shard_map/transpose | solution.py:348

commit v6 on v4

--- a/solution.py
+++ b/solution.py
@@ -129,8 +129,8 @@
         hit = hits[0] if len(hits) == 1 else jnp.concatenate(hits, axis=0)
         return jnp.dot(hit.astype(BF16), hist_ref[p], preferred_element_type=F32)
 
-    def share_of_steps(steps):
-        for i in range(0, patches, 2):
+    def share_of_steps(steps, first_patch=0, last_patch=patches):
+        for i in range(first_patch, last_patch, 2):
             a = stored_share(i, steps)
             b = stored_share(i + 1, steps)
             for k, step in enumerate(steps):
@@ -139,13 +139,14 @@
                     both = jnp.concatenate([a[r : r + loc], b[r : r + loc]], axis=0)
                     hsend[step, d, i * loc : (i + 2) * loc, :] = both.astype(BF16)
 
-    def hist_copy(step, off):
+    def hist_copy(step, off, half):
         dest = slab_peer(off)
-        return pltpu.make_async_remote_copy(
-            src_ref=hsend.at[step, dest],
-            dst_ref=hrecv.at[step, off],
-            send_sem=h_send_sem.at[step],
-            recv_sem=h_recv_sem.at[step],
+        part = pl.ds(half * (rows // 2), rows // 2)
+        return pltpu.make_async_remote_copy(
+            src_ref=hsend.at[step, dest, part],
+            dst_ref=hrecv.at[step, off, part],
+            send_sem=h_send_sem.at[step, half],
+            recv_sem=h_recv_sem.at[step, half],
             device_id={"patch": me, "slab": dest},
             device_id_type=MESH,
         )
@@ -192,17 +193,32 @@
         wm[j] = jnp.where(j < band_t, weights[:, j, :].T, 0.0)
     small[2].wait()
     small[3].wait()
-    share_of_steps([0])
+    share_of_steps([0], 0, patches // 2)
 
     pl.semaphore_wait(barrier, n_patch + n_slab - 2)
 
-    def send_hist(step):
+    def send_hist(step, half):
         for off in range(n_slab - 1, 0, -1):
-            hist_copy(step, off).start()
-
-    send_hist(0)
+            hist_copy(step, off, half).start()
+
+    def hist_of(step, half):
+        part = pl.ds(half * (rows // 2), rows // 2)
+        slots = hrecv.at[step, pl.ds(1, n_slab - 1), part]
+        return pltpu.make_async_remote_copy(
+            src_ref=slots,
+            dst_ref=slots,
+            send_sem=h_send_sem.at[step, half],
+            recv_sem=h_recv_sem.at[step, half],
+            device_id={"patch": me, "slab": slab_peer(1)},
+            device_id_type=MESH,
+        )
+
+    send_hist(0, 0)
+    share_of_steps([0], patches // 2)
+    send_hist(0, 1)
     share_of_steps([1])
-    send_hist(1)
+    for half in range(2):
+        send_hist(1, half)
 
     mine = pl.ds(pl.multiple_of(slab * loc, loc), loc)
 
@@ -217,21 +233,23 @@
             acc = jnp.where(first == d - j, taps[j], acc)
         recent_w[d] = jnp.broadcast_to(acc, (rows, src))
     target = lax.broadcasted_iota(jnp.int32, (rows, total), 1)
-    onehot[...] = (target == column(obs_t[mine, :])).astype(F32).T.astype(BF16)
+    hit = (target == column(obs_t[mine, :])).astype(F32).T.astype(BF16)
+    onehot[...] = jnp.concatenate([hit, hit], axis=1)
     for step in range(STEPS):
         inc[step] = inc_ref[:, step, :]
 
     def repeat(a):
         return jnp.broadcast_to(a[:, None, :], (patches, loc, src)).reshape(rows, src)
 
-    def prepare(step):
-        all_of(step, hrecv, h_send_sem, h_recv_sem).wait_recv()
-        acc = hsend[step, slab].astype(F32)
+    def prepare(step, half):
+        hist_of(step, half).wait_recv()
+        part = pl.ds(half * (rows // 2), rows // 2)
+        acc = hsend[step, slab, part, :].astype(F32)
         for off in range(1, n_slab):
-            acc = acc + hrecv[step, off].astype(F32)
+            acc = acc + hrecv[step, off, part, :].astype(F32)
         for d in range(2, step + 1):
-            acc = acc + recent_w[d] * repeat(amps[step - d])
-        pre[...] = acc
+            acc = acc + recent_w[d, part, :] * repeat(amps[step - d])[part.start : part.start + part.size]
+        pre[part, :] = acc
 
     for load in loads:
         load.wait()
@@ -246,26 +264,25 @@
 
     turn(coup, coup_t)
     turn(inv, inv_t)
-    prepare(0)
 
     for step in range(STEPS):
-        driven = pre[...]
         if step > 0:
-            driven = driven + recent_w[1] * repeat(amps[step - 1])
-        pre[...] = driven
+            pre[...] = pre[...] + recent_w[1] * repeat(amps[step - 1])
 
         def couple(p, carry):
             at = pl.ds(pl.multiple_of(p * 2 * loc, 2 * loc), 2 * loc)
             coupled[at, :] = own_blocks(pre[at, :], coup_t[p])
             return carry
 
-        lax.fori_loop(0, patches // 2, couple, 0, unroll=True)
+        for half in range(2):
+            if step == 0:
+                prepare(0, half)
+            lax.fori_loop(half * patches // 4, (half + 1) * patches // 4, couple, 0, unroll=True)
         whole = coupled[...]
         high = whole.astype(BF16)
         low = (whole - high.astype(F32)).astype(BF16)
-        field = jnp.dot(onehot[...], high, preferred_element_type=F32) + jnp.dot(
-            onehot[...], low, preferred_element_type=F32
-        )
+        both = jnp.concatenate([high, low], axis=0)
+        field = jnp.dot(onehot[...], both, preferred_element_type=F32)
         fsend[step] = field.astype(BF16).reshape(n_patch, patches, src)
         for off in range(n_patch - 1, 0, -1):
             field_copy(step, off).start()
@@ -279,10 +296,12 @@
         for off in range(n_slab - 1, 0, -1):
             slab_copy(step, off).start()
         if step + 1 < STEPS:
-            prepare(step + 1)
+            for half in range(2):
+                prepare(step + 1, half)
         all_of(step, zbuf, z_send_sem, z_recv_sem).wait_recv()
         if step + 2 < STEPS:
-            send_hist(step + 2)
+            for half in range(2):
+                send_hist(step + 2, half)
         scattered = zbuf[step, lax.rem(slab, n_slab)].astype(F32)
         for t in range(1, n_slab):
             scattered = scattered + zbuf[step, lax.rem(slab + n_slab - t, n_slab)].astype(F32)
@@ -292,7 +311,8 @@
         amps[step] = amp.astype(F32)
 
     for step in range(STEPS):
-        all_of(step, hsend, h_send_sem, h_recv_sem).wait_send()
+        for half in range(2):
+            hist_of(step, half).wait_send()
         all_of(step, fsend, f_send_sem, f_recv_sem).wait_send()
         all_of(step, zbuf, z_send_sem, z_recv_sem).wait_send()
 
@@ -309,7 +329,7 @@
     dma = pltpu.SemaphoreType.DMA
     out = pl.pallas_call(
         functools.partial(march, n_patch, n_slab),
-        out_shape=jax.ShapeDtypeStruct((STEPS, patches, src), BF16),
+        out_shape=pltpu.VMEM((STEPS, patches, src), BF16),
         in_specs=[hbm] * 6,
         out_specs=vmem,
         scratch_shapes=[
@@ -325,7 +345,7 @@
             pltpu.VMEM((pairs, patches), jnp.int32),
             pltpu.VMEM((WMAX, pairs, patches), F32),
             pltpu.VMEM((STEPS, rows, src), F32),
-            pltpu.VMEM((total, rows), BF16),
+            pltpu.VMEM((total, 2 * rows), BF16),
             pltpu.VMEM((STEPS, patches, src), F32),
             pltpu.VMEM((STEPS, patches, src), F32),
             pltpu.VMEM((rows, src), F32),
@@ -336,15 +356,15 @@
             pltpu.VMEM((STEPS, n_patch, patches, src), BF16),
             pltpu.VMEM((STEPS, n_slab, patches, src), BF16),
             dma((9,)),
-            dma((STEPS,)),
-            dma((STEPS,)),
+            dma((STEPS, 2)),
+            dma((STEPS, 2)),
             dma((STEPS,)),
             dma((STEPS,)),
             dma((STEPS,)),
             dma((STEPS,)),
         ],
         compiler_params=pltpu.CompilerParams(
-            collective_id=0, has_side_effects=True, vmem_limit_bytes=63 * 1024 * 1024
+            collective_id=0, has_side_effects=True, vmem_limit_bytes=62 * 1024 * 1024
         ),
     )(
         history,

time: 44.2 us -> 42.7 us (0.966)
  local copies, waits for them, and re-layouts: 1.33 us -> 0.61 us
  Pallas kernels: 42.6 us -> 41.9 us
    transpose x1, local copies, waits for them, and re-layouts: 1.33 us -> 0.61 us  [on_device(): return out.transpose(1, 0, 2)]
    pallas_call x1, Pallas kernels: 42.6 us -> 41.9 us  [on_device(): pl.pallas_call(functools.partial(march, n_patch, n_slab), out_shape=pltpu...]
where the time goes in v6:
time: 42.7 us; the launch traced here: 42.6 us
  Pallas kernels  41.9 us (98%)
  local copies, waits for them, and re-layouts  0.61 us (1%)
    pallas_call x1, Pallas kernels, on_device(): pl.pallas_call(functools.partial(march, n_patch, n_slab), out_shape=pltpu...  41.9 us

profile of v6, /device:TPU:0, one launch (start us, length us, event | category | flops | bytes accessed | tf_op | source)
XLA Modules:
  0.0 42.6 jit_solution(1450801747035433409)
XLA Ops:
  0.0 41.9 %shard_map.64 = bf16[4,16,128]{2,1,0:T(8,128)(2,1)S(1)} custom-call(bf16[16,64,128]{2,1,0:T(8,128)(2,1)} %hist_hbm.1, bf16[16,4,32]{2,1,0:T(4,128)(2,1)} %bitcast.9, s32[3,16,32]{2,1,0:T(8,128)} %bitcast.8, bf16[16,1024,128]{2,1,0:T(8,128)(2,1)} %bitcast.6, bf16[2,1024,128]{2,1,0:T(8,128)(2,1)} %bitcast.7, f32[16,4,128]{2,1,0:T(4,128)} %inc_hbm.1), custom_call_target="tpu_custom_call" | custom-call | tf_op jit(solution)/shard_map/pallas_call | solution.py:330
  41.9 0.6 %copy.7 = bf16[16,4,128]{2,1,0:T(4,128)(2,1)} copy(bf16[16,4,128]{2,0,1:T(8,128)(2,1)S(1)} %bitcast.5) | data formatting | bytes 32768 | tf_op jit(solution)/shard_map/transpose | solution.py:377

commit v7 on v6

--- a/solution.py
+++ b/solution.py
@@ -56,6 +56,8 @@
     amps,
     pre,
     coupled,
+    folded,
+    ready,
     hsend,
     hrecv,
     fsend,
@@ -265,20 +267,39 @@
     turn(coup, coup_t)
     turn(inv, inv_t)
 
+    def couple(matrices, into, begin, end):
+        def one(g, carry):
+            at = pl.ds(pl.multiple_of(g * 2 * loc, 2 * loc), 2 * loc)
+            into[at, :] = own_blocks(pre[at, :], matrices[g])
+            return carry
+
+        lax.fori_loop(begin, end, one, 0, unroll=True)
+
+    def fold():
+        count = patches // 2
+        for p in range(patches):
+            h, r = p // count, p % count
+            left = inv_t[0, h * src : (h + 1) * src, r * src : (r + 1) * src]
+            at = pl.ds((p % 2) * src, src)
+            product = jnp.dot(left, coup_t[p // 2, at, :], preferred_element_type=F32)
+            folded[p // 2, at, :] = product.astype(BF16)
+
+    def finish(step, drive):
+        amp = own_blocks(drive, inv_t[0]).astype(BF16)
+        out_ref[step] = amp
+        amps[step] = amp.astype(F32)
+
+    drive = None
     for step in range(STEPS):
         if step > 0:
-            pre[...] = pre[...] + recent_w[1] * repeat(amps[step - 1])
-
-        def couple(p, carry):
-            at = pl.ds(pl.multiple_of(p * 2 * loc, 2 * loc), 2 * loc)
-            coupled[at, :] = own_blocks(pre[at, :], coup_t[p])
-            return carry
-
-        for half in range(2):
-            if step == 0:
+            pre[...] = repeat(drive)
+            couple(folded, coupled, 0, patches // 2)
+            whole = ready[...] + recent_w[1] * coupled[...]
+        else:
+            for half in range(2):
                 prepare(0, half)
-            lax.fori_loop(half * patches // 4, (half + 1) * patches // 4, couple, 0, unroll=True)
-        whole = coupled[...]
+                couple(coup_t, coupled, half * patches // 4, (half + 1) * patches // 4)
+            whole = coupled[...]
         high = whole.astype(BF16)
         low = (whole - high.astype(F32)).astype(BF16)
         both = jnp.concatenate([high, low], axis=0)
@@ -287,7 +308,9 @@
         for off in range(n_patch - 1, 0, -1):
             field_copy(step, off).start()
         if step == 0:
-            share_of_steps(list(range(2, STEPS)))
+            fold()
+        else:
+            finish(step - 1, drive)
         all_of(step, frecv, f_send_sem, f_recv_sem).wait_recv()
         share = fsend[step, me].astype(F32)
         for off in range(1, n_patch):
@@ -295,9 +318,12 @@
         zbuf[step, 0] = share.astype(BF16)
         for off in range(n_slab - 1, 0, -1):
             slab_copy(step, off).start()
+        if step == 0:
+            share_of_steps(list(range(2, STEPS)))
         if step + 1 < STEPS:
             for half in range(2):
                 prepare(step + 1, half)
+            couple(coup_t, ready, 0, patches // 2)
         all_of(step, zbuf, z_send_sem, z_recv_sem).wait_recv()
         if step + 2 < STEPS:
             for half in range(2):
@@ -305,10 +331,8 @@
         scattered = zbuf[step, lax.rem(slab, n_slab)].astype(F32)
         for t in range(1, n_slab):
             scattered = scattered + zbuf[step, lax.rem(slab + n_slab - t, n_slab)].astype(F32)
-        drive = inc[step] - scattered
-        amp = own_blocks(drive, inv_t[0]).astype(BF16)
-        out_ref[step] = amp
-        amps[step] = amp.astype(F32)
+        drive = (inc[step] - scattered).astype(BF16).astype(F32)
+    finish(STEPS - 1, drive)
 
     for step in range(STEPS):
         for half in range(2):
@@ -350,6 +374,8 @@
             pltpu.VMEM((STEPS, patches, src), F32),
             pltpu.VMEM((rows, src), F32),
             pltpu.VMEM((rows, src), F32),
+            pltpu.VMEM((patches // 2, 2 * src, loc * src), BF16),
+            pltpu.VMEM((rows, src), F32),
             pltpu.VMEM((STEPS, n_slab, rows, src), BF16),
             pltpu.VMEM((STEPS, n_slab, rows, src), BF16),
             pltpu.VMEM((STEPS, n_patch, patches, src), BF16),

time: 42.7 us -> 42.2 us (0.988)
    pallas_call x1, Pallas kernels: 41.9 us -> 41.5 us  [on_device(): pl.pallas_call(functools.partial(march, n_patch, n_slab), out_shape=pltpu...]
where the time goes in v7:
time: 42.2 us; the launch traced here: 42.1 us
  Pallas kernels  41.5 us (98%)
  local copies, waits for them, and re-layouts  0.61 us (1%)
    pallas_call x1, Pallas kernels, on_device(): pl.pallas_call(functools.partial(march, n_patch, n_slab), out_shape=pltpu...  41.5 us

profile of v7, /device:TPU:0, one launch (start us, length us, event | category | flops | bytes accessed | tf_op | source)
XLA Modules:
  0.0 42.1 jit_solution(7940318723133469584)
XLA Ops:
  0.0 41.5 %shard_map.64 = bf16[4,16,128]{2,1,0:T(8,128)(2,1)S(1)} custom-call(bf16[16,64,128]{2,1,0:T(8,128)(2,1)} %hist_hbm.1, bf16[16,4,32]{2,1,0:T(4,128)(2,1)} %bitcast.9, s32[3,16,32]{2,1,0:T(8,128)} %bitcast.8, bf16[16,1024,128]{2,1,0:T(8,128)(2,1)} %bitcast.6, bf16[2,1024,128]{2,1,0:T(8,128)(2,1)} %bitcast.7, f32[16,4,128]{2,1,0:T(4,128)} %inc_hbm.1), custom_call_target="tpu_custom_call" | custom-call | tf_op jit(solution)/shard_map/pallas_call | solution.py:354
  41.5 0.6 %copy.7 = bf16[16,4,128]{2,1,0:T(4,128)(2,1)} copy(bf16[16,4,128]{2,0,1:T(8,128)(2,1)S(1)} %bitcast.5) | data formatting | bytes 32768 | tf_op jit(solution)/shard_map/transpose | solution.py:403

commit v8 on v7

--- a/solution.py
+++ b/solution.py
@@ -227,18 +227,20 @@
     def column(x):
         return jnp.concatenate([x[:, p : p + 1] for p in range(patches)], axis=0)
 
-    first = column(first_t[mine, :])
-    taps = [column(wm[j, mine, :]) for j in range(min(WMAX, STEPS - 1))]
-    for d in range(1, STEPS):
-        acc = jnp.zeros((rows, 1), F32)
-        for j in range(min(WMAX, d)):
-            acc = jnp.where(first == d - j, taps[j], acc)
-        recent_w[d] = jnp.broadcast_to(acc, (rows, src))
     target = lax.broadcasted_iota(jnp.int32, (rows, total), 1)
     hit = (target == column(obs_t[mine, :])).astype(F32).T.astype(BF16)
     onehot[...] = jnp.concatenate([hit, hit], axis=1)
-    for step in range(STEPS):
-        inc[step] = inc_ref[:, step, :]
+
+    def recent_tables():
+        first = column(first_t[mine, :])
+        taps = [column(wm[j, mine, :]) for j in range(min(WMAX, STEPS - 1))]
+        for d in range(1, STEPS):
+            acc = jnp.zeros((rows, 1), F32)
+            for j in range(min(WMAX, d)):
+                acc = jnp.where(first == d - j, taps[j], acc)
+            recent_w[d] = jnp.broadcast_to(acc, (rows, src))
+        for step in range(STEPS):
+            inc[step] = inc_ref[:, step, :]
 
     def repeat(a):
         return jnp.broadcast_to(a[:, None, :], (patches, loc, src)).reshape(rows, src)
@@ -265,7 +267,6 @@
                     turned[g, h * src : (h + 1) * src, r * src : (r + 1) * src] = block.T
 
     turn(coup, coup_t)
-    turn(inv, inv_t)
 
     def couple(matrices, into, begin, end):
         def one(g, carry):
@@ -308,9 +309,12 @@
         for off in range(n_patch - 1, 0, -1):
             field_copy(step, off).start()
         if step == 0:
+            turn(inv, inv_t)
             fold()
         else:
             finish(step - 1, drive)
+            if step + 2 < STEPS:
+                share_of_steps([step + 2])
         all_of(step, frecv, f_send_sem, f_recv_sem).wait_recv()
         share = fsend[step, me].astype(F32)
         for off in range(1, n_patch):
@@ -319,7 +323,8 @@
         for off in range(n_slab - 1, 0, -1):
             slab_copy(step, off).start()
         if step == 0:
-            share_of_steps(list(range(2, STEPS)))
+            recent_tables()
+            share_of_steps([2])
         if step + 1 < STEPS:
             for half in range(2):
                 prepare(step + 1, half)

time: 42.2 us -> 42.2 us (level)
  no operation moved by 1% of the time
where the time goes in v8:
time: 42.2 us; the launch traced here: 42.1 us
  Pallas kernels  41.5 us (98%)
  local copies, waits for them, and re-layouts  0.61 us (1%)
    pallas_call x1, Pallas kernels, on_device(): pl.pallas_call(functools.partial(march, n_patch, n_slab), out_shape=pltpu...  41.5 us

profile of v8, /device:TPU:0, one launch (start us, length us, event | category | flops | bytes accessed | tf_op | source)
XLA Modules:
  0.0 42.1 jit_solution(9963037709338639411)
XLA Ops:
  0.0 41.5 %shard_map.64 = bf16[4,16,128]{2,1,0:T(8,128)(2,1)S(1)} custom-call(bf16[16,64,128]{2,1,0:T(8,128)(2,1)} %hist_hbm.1, bf16[16,4,32]{2,1,0:T(4,128)(2,1)} %bitcast.9, s32[3,16,32]{2,1,0:T(8,128)} %bitcast.8, bf16[16,1024,128]{2,1,0:T(8,128)(2,1)} %bitcast.6, bf16[2,1024,128]{2,1,0:T(8,128)(2,1)} %bitcast.7, f32[16,4,128]{2,1,0:T(4,128)} %inc_hbm.1), custom_call_target="tpu_custom_call" | custom-call | tf_op jit(solution)/shard_map/pallas_call | solution.py:359
  41.5 0.6 %copy.7 = bf16[16,4,128]{2,1,0:T(4,128)(2,1)} copy(bf16[16,4,128]{2,0,1:T(8,128)(2,1)S(1)} %bitcast.5) | data formatting | bytes 32768 | tf_op jit(solution)/shard_map/transpose | solution.py:408
